TPU v7x, 32 devices: a whole 2x2x4 slice. The times are simulated.
32 devices in a mesh: ens: 2 (over x), lat: 16 (over z, y, core).
Axes of the slice: x: 2, y: 2, z: 4, core: 2. Of those that a mesh axis runs over, the one named last changes fastest.
Arguments:
- state_field: bfloat16 [64, 768, 320], P(('ens', 'lat')), parts along dimension 0, may hold values from -6 to 6
- noise_field: bfloat16 [64, 768, 320], P(('ens', 'lat')), parts along dimension 0, may hold values from -6 to 6
- noise_scale: float32 [320], replicated, may hold values from 0.1 to 1
- basis_filter: float32 [3, 32, 3, 3], replicated, may hold values from -1 to 1
- row_index: int32 [32, 3], replicated, may hold values from 0 to 31, as said below
- basis_weight: float32 [3, 320], replicated, may hold values from -2 to 2
- spectral_gain: float32 [80, 320], replicated, may hold values from -1.5 to 1.5
- cotangent: bfloat16 [64, 768, 320], P(('ens', 'lat')), parts along dimension 0, may hold values from -18 to 18
Outputs:
- field_grad: bfloat16 [64, 768, 320], P(('ens', 'lat')), parts along dimension 0
- basis_grad: float32 [6, 320], P('ens'), parts along dimension 0
- gain_grad: float32 [160, 320], P('ens'), parts along dimension 0
- scale_grad: float32 [640], P('ens'), parts along dimension 0
There are 2 independent parts, one for each index of `ens`. A program takes and returns all parts, laid end to end along the dimension named above; an argument that names none is the same for every part. Nothing has to cross between parts.
Inputs may be any that keep to these rules, and one draw needn't show every extreme that they name: row_index[i, 1] = i; row_index[i, 0] lies in i - 2 to i - 1 and row_index[i, 2] in i + 1 to i + 2, each clipped to the grid.
All inputs are finite; a program needn't handle non-finite values.
Results may differ from a plain program's by a relative error of at most 0.0091.
Values may be sent and summed in bfloat16 or wider, within the bound.
A program may use at most 128 MiB of HBM per device.

v0:
```python
import jax
import jax.numpy as jnp
from jax import lax
from jax.sharding import PartitionSpec as P


def padded_2(array, sides, width):
    for axis, dim in sides:
        devices, length = (lax.axis_size(axis), array.shape[dim])
        up = [(i, (i + 1) % devices) for i in range(devices - 1)]
        down = [(j, i) for i, j in up]
        last = lax.slice_in_dim(array, length - width, length, axis=dim)
        first = lax.slice_in_dim(array, 0, width, axis=dim)
        before = lax.ppermute(last, axis, up)
        after = lax.ppermute(first, axis, down)
        array = jnp.concatenate([before, array, after], axis=dim)
    return array


def shifted(block, axis, distance):
    devices = range(lax.axis_size(axis))
    route = [(i - distance, i) for i in devices if i - distance in devices]
    return lax.ppermute(block, axis, route)


def legendre_table(orders_used, lat_count, degree_count):
    row_float = jnp.arange(lat_count, dtype=jnp.float32)
    colatitude = jnp.pi * (row_float + 0.5) / lat_count
    cos_lat = jnp.cos(colatitude)
    sine_lat = jnp.sin(colatitude)
    counter = jnp.arange(1, degree_count + 1, dtype=jnp.float32)
    log_terms = 0.5 * jnp.log((2.0 * counter + 1.0) / (2.0 * counter))
    partial_sum = jnp.sum(
        jnp.where(counter[None, :] <= orders_used[:, None], log_terms[None, :], 0.0), axis=1
    )
    log_start = (
        0.5 * jnp.log(1.0 / (4.0 * jnp.pi))
        + partial_sum[:, None]
        + orders_used[:, None] * jnp.log(sine_lat)[None, :]
    )
    diagonal_start = jnp.exp(log_start)
    order_col = orders_used[:, None]

    def advance(carried, degree):
        prev_one, prev_two = carried
        degree_float = degree.astype(jnp.float32)
        ratio_a = jnp.sqrt(
            (4.0 * degree_float * degree_float - 1.0)
            / jnp.maximum(degree_float * degree_float - order_col * order_col, 1.0)
        )
        ratio_b = jnp.sqrt(
            jnp.maximum((degree_float - 1.0) ** 2 - order_col * order_col, 0.0)
            / jnp.maximum(4.0 * (degree_float - 1.0) ** 2 - 1.0, 1.0)
        )
        general = ratio_a * (cos_lat[None, :] * prev_one - ratio_b * prev_two)
        current = jnp.where(
            degree_float < order_col,
            0.0,
            jnp.where(degree_float == order_col, diagonal_start, general),
        )
        return ((current, prev_one), current)

    blank_rows = jnp.zeros((orders_used.shape[0], lat_count), jnp.float32)
    _, stacked = lax.scan(
        advance, (blank_rows, blank_rows), jnp.arange(degree_count, dtype=jnp.int32), unroll=16
    )
    return jnp.transpose(stacked, (1, 0, 2))


def quadrature(lat_count):
    row_float = jnp.arange(lat_count, dtype=jnp.float32)
    return jnp.pi / lat_count * jnp.sin(jnp.pi * (row_float + 0.5) / lat_count)


def transform_tables(lon_count, mode_count):
    points = jnp.arange(lon_count, dtype=jnp.int32)
    orders = jnp.arange(mode_count, dtype=jnp.int32)
    phases = (points[:, None] * orders[None, :] % lon_count).astype(jnp.float32) * (
        2.0 * jnp.pi / lon_count
    )
    forward = jnp.stack([jnp.cos(phases), -jnp.sin(phases)], axis=-1) * (2.0 * jnp.pi / lon_count)
    weight_m = jnp.where(orders == 0, 1.0, 2.0).astype(jnp.float32)
    inverse = jnp.stack([jnp.cos(phases), -jnp.sin(phases)], axis=-1) * weight_m[None, :, None]
    return (forward.astype(jnp.bfloat16), jnp.transpose(inverse, (1, 2, 0)).astype(jnp.bfloat16))


def gelu_tanh(pre_act):
    return jax.nn.gelu(pre_act, approximate=True)


def to_pencil(values_band):
    return lax.all_to_all(values_band, "lat", split_axis=1, concat_axis=0, tiled=True)


def to_band(values_pencil):
    return lax.all_to_all(values_pencil, "lat", split_axis=0, concat_axis=1, tiled=True)


def body(
    state_field,
    noise_field,
    noise_scale,
    basis_filter,
    row_index,
    basis_weight,
    spectral_gain,
    cotangent,
):
    highest = lax.Precision.HIGHEST
    row_span = state_field.shape[0]
    lon_count = state_field.shape[1]
    devices = lax.axis_size("lat")
    position = lax.axis_index("lat")
    total_lat = row_span * devices
    degree_count = spectral_gain.shape[0]
    modes_each = degree_count // devices
    tap_count = row_index.shape[1]
    first_row = position * row_span
    start_field = (
        state_field.astype(jnp.float32) + noise_scale * noise_field.astype(jnp.float32)
    ).astype(jnp.bfloat16)
    padded = padded_2(start_field, (("lat", 0),), row_span)
    local_rows = lax.dynamic_slice_in_dim(row_index, first_row, row_span, 0) - (
        first_row - row_span
    )
    local_filter = lax.dynamic_slice_in_dim(basis_filter, first_row, row_span, 1)
    coeffs = jnp.einsum("kits,kc->itsc", local_filter, basis_weight, precision=highest)
    local_sum = jnp.zeros(start_field.shape, jnp.float32)
    picked_rows = []
    for tap_no in range(tap_count):
        picked = jnp.take(padded, local_rows[:, tap_no], axis=0)
        picked_rows.append(picked)
        for offset in range(3):
            local_sum = local_sum + coeffs[:, tap_no, offset, None, :] * jnp.roll(
                picked, 1 - offset, axis=1
            ).astype(jnp.float32)
    forward, inverse = transform_tables(lon_count, degree_count)
    orders_here = (position * modes_each + jnp.arange(modes_each, dtype=jnp.int32)).astype(
        jnp.float32
    )
    legendre = legendre_table(orders_here, total_lat, degree_count)
    analysis = (legendre * quadrature(total_lat)[None, None, :]).astype(jnp.bfloat16)
    synthesis = legendre.astype(jnp.bfloat16)
    spectra = jnp.einsum(
        "jnc,nmr->jmrc", start_field, forward, preferred_element_type=jnp.float32
    ).astype(jnp.bfloat16)
    pencil = to_pencil(spectra)
    coefficients = jnp.einsum(
        "mlj,jmrc->mlrc", analysis, pencil, preferred_element_type=jnp.float32
    )
    filtered = (spectral_gain[None, :, None, :] * coefficients).astype(jnp.bfloat16)
    returned_pencil = jnp.einsum(
        "mlj,mlrc->jmrc", synthesis, filtered, preferred_element_type=jnp.float32
    ).astype(jnp.bfloat16)
    returned = to_band(returned_pencil)
    spectral_part = jnp.einsum(
        "jmrc,mrn->jnc", returned, inverse, preferred_element_type=jnp.float32
    )
    pre = local_sum + spectral_part
    _, pullback = jax.vjp(gelu_tanh, pre)
    grad_pre = pullback(cotangent.astype(jnp.float32))[0].astype(jnp.bfloat16)
    grad_wide = grad_pre.astype(jnp.float32)
    grad_returned = jnp.einsum(
        "jnc,mrn->jmrc", grad_pre, inverse, preferred_element_type=jnp.float32
    ).astype(jnp.bfloat16)
    grad_coeff = jnp.einsum(
        "mlj,jmrc->mlrc", synthesis, to_pencil(grad_returned), preferred_element_type=jnp.float32
    )
    gain_part = jnp.sum(coefficients * grad_coeff, axis=(0, 2))
    grad_filtered = (spectral_gain[None, :, None, :] * grad_coeff).astype(jnp.bfloat16)
    grad_pencil = jnp.einsum(
        "mlj,mlrc->jmrc", analysis, grad_filtered, preferred_element_type=jnp.float32
    ).astype(jnp.bfloat16)
    grad_spectra = to_band(grad_pencil)
    spectral_back = jnp.einsum(
        "jmrc,nmr->jnc", grad_spectra, forward, preferred_element_type=jnp.float32
    )
    slot_ids = jnp.arange(3 * row_span, dtype=jnp.int32)
    gathered = jnp.zeros((3 * row_span, lon_count, grad_pre.shape[2]), jnp.float32)
    for tap_no in range(tap_count):
        spread = jnp.zeros(grad_wide.shape, jnp.float32)
        for offset in range(3):
            spread = spread + coeffs[:, tap_no, offset, None, :] * jnp.roll(
                grad_wide, offset - 1, axis=1
            )
        onehot = (local_rows[:, tap_no][None, :] == slot_ids[:, None]).astype(jnp.float32)
        gathered = gathered + jnp.einsum("ei,inc->enc", onehot, spread, precision=highest)
    local_back = gathered[row_span : 2 * row_span]
    for step_dir in (1, -1):
        rim_rows = gathered[2 * row_span :] if step_dir == 1 else gathered[:row_span]
        local_back = local_back + shifted(rim_rows.astype(jnp.bfloat16), "lat", step_dir).astype(
            rim_rows.dtype
        )
    products = []
    for tap_no in range(tap_count):
        picked = picked_rows[tap_no]
        tap_products = []
        for offset in range(3):
            tap_products.append(
                jnp.sum(
                    grad_wide * jnp.roll(picked, 1 - offset, axis=1).astype(jnp.float32), axis=1
                )
            )
        products.append(jnp.stack(tap_products, axis=1))
    products = jnp.stack(products, axis=1)
    basis_part = jnp.einsum("kits,itsc->kc", local_filter, products, precision=highest)
    grad_sum = spectral_back + local_back
    scale_part = jnp.sum(grad_sum * noise_field.astype(jnp.float32), axis=(0, 1))
    basis_grad, gain_grad, scale_grad = lax.psum((basis_part, gain_part, scale_part), "lat")
    return (grad_sum.astype(jnp.bfloat16), basis_grad, gain_grad, scale_grad)


def solution(mesh):
    return jax.shard_map(
        body,
        mesh=mesh,
        in_specs=(
            P(("ens", "lat"), None, None),
            P(("ens", "lat"), None, None),
            P(),
            P(),
            P(),
            P(),
            P(),
            P(("ens", "lat"), None, None),
        ),
        out_specs=(P(("ens", "lat"), None, None), P("ens", None), P("ens", None), P("ens")),
        check_vma=False,
    )
```

profile of v0, /device:TPU:8, one launch (start us, length us, event | category | flops | bytes accessed | tf_op | source)
XLA Modules:
  0.0 302.0 jit_solution(2636201206000656243)
XLA Ops:
  7.2 1.9 fusion.48
  9.1 2.9 collective-permute-start.1
  12.0 1.9 collective-permute-start
  13.9 1.0 sine_negate_fusion
  14.9 0.5 fusion.89
  15.4 0.9 copy.75
  16.3 6.5 %all-to-all-start = ((bf16[2,80,2,320]{3,0,2,1:T(2,128)(2,1)}), bf16[2,80,2,320]{3,0,2,1:T(2,128)(2,1)S(1)}, u32[]{:S(2)}, u32[]{:S(2)}) async-start(bf16[2,80,2,320]{3,0,2,1:T(2,128)(2,1)} %copy.75), calls=%async_computation | async-start | bytes 491520 | tf_op jit(solution)/shard_map/all_to_all | solution.py:92
  23.0 0.6 slice_bitcast_fusion.2
  23.5 0.5 compare_and_fusion.2
  24.3 0.6 pad_clamp_fusion.2
  25.4 0.6 fusion.164
  26.0 64.4 %while.21 = (s32[]{:T(128)}, f32[5,32]{1,0:T(8,128)S(1)}, f32[5,32]{1,0:T(8,128)S(1)}, f32[5,16,5,32]{3,2,1,0:T(8,128)S(1)}, s32[5,16]{1,0:T(8,128)S(1)}, /*inde...) while((s32[]{:T(128)}, f32[5,32]{1,0:T(8,128)S(1)}, ...), condition=%wide.region_2.3_spmd.clone.clone.clone.clone, body=%wide.region_1.2_spmd.clone.clone.clone.clone.sunk | while | flops 36626 | bytes 474266 | solution.py:64
  26.1 0.7 fusion.170
  38.9 0.7 fusion.170
  51.8 0.7 fusion.170
  64.7 0.7 fusion.170
  77.6 0.7 fusion.170
  90.4 0.6 pad_clamp_fusion
  91.6 0.4 fusion.121
  92.1 1.0 copy-done.2
  93.4 0.9 copy.78
  94.2 6.3 %all-to-all-start.1 = ((bf16[32,5,2,320]{3,2,1,0:T(2,128)(2,1)}), bf16[32,5,2,320]{3,2,1,0:T(2,128)(2,1)S(1)}, u32[]{:S(2)}, u32[]{:S(2)}) async-start(bf16[32,5,2,320]{3,2,1,0:T(2,128)(2,1)} %copy.78), calls=%async_computation.1 | async-start | bytes 491520 | tf_op jit(solution)/shard_map/all_to_all | solution.py:96
  100.5 0.5 compare_select_fusion.3
  101.0 0.6 pad_clamp_fusion.1
  101.7 0.6 copy_bitcast_fusion.6
  102.2 5.7 %all-to-all-done.1 = bf16[32,5,2,320]{3,2,1,0:T(2,128)(2,1)S(1)} async-done(((bf16[32,5,2,320]{3,2,1,0:T(2,128)(2,1)}), bf16[32,5,2,320]{3,2,1,0:T(2,128)(2,1)S(1)}, u32[]{:S(2)}, u32[]{:S(2)}) %all-to-all-start.1) | async-done | bytes 204832 | tf_op jit(solution)/shard_map/all_to_all | solution.py:96
  107.9 0.9 copy.79
  108.8 0.9 copy-done.11
  109.7 2.1 pad_maximum_fusion
  111.9 1.7 gather_fusion.2
  113.5 1.7 gather_fusion.1
  115.2 1.7 broadcast_select_fusion
  117.0 0.9 fusion.162
  117.9 1.8 fusion.163
  119.7 0.8 fusion.160
  120.5 1.8 fusion.161
  122.3 1.7 gather_fusion
  123.9 1.5 broadcast_select_fusion.2
  125.7 0.5 fusion.159
  126.6 0.3 copy-done.5
  127.5 0.3 copy-done.13
  127.8 9.1 %fusion.70 = (f32[2,320]{1,0:T(2,128)}, f32[2,320]{1,0:T(2,128)}, f32[2,320]{1,0:T(2,128)}, f32[2,320]{1,0:T(2,128)}, f32[2,320]{1,0:T(2,128)}, /*index=5*/f32[2...) fusion(bf16[2,767,320]{1,2,0:T(8,128)(2,1)S(1)} %get-tuple-element.541, ...), kind=kOutput, calls=%fused_computation.186 | convolution fusion | flops 199428480 | bytes 11556160 | tf_op jit(solution)/shard_map/jmrc,mrn->jnc/dot_general | solution.py:156
  136.9 0.5 fusion.90
  137.5 0.5 fusion.156
  138.1 1.0 fusion.69
  139.1 3.4 %fusion.65 = (f32[2,768,320]{1,2,0:T(8,128)}, f32[2,768,320]{1,2,0:T(8,128)}) fusion(bf16[2,768,320]{1,2,0:T(8,128)(2,1)S(1)} %get-tuple-element.568, f32[2,320]{1,0:T(2,128)S(1)} %get-tuple-element.583, f32[2,320]{1,0:T(2,128)S(1)} %copy-done.23, f32[2,320]{1,0:T(2,128)S(1)} %bitcast.470, f32[2,767,320]{1,2,0:T(8,128)S(1)} %get-tuple-element.536, ...), kind=kLoop, calls=%fused_computation.181 | loop fusion | flops 6389760 | bytes 8862720 | tf_op jit(solution)/shard_map/add | solution.py:183
  142.5 0.9 copy.81
  143.4 6.5 %all-to-all-start.2 = ((bf16[2,80,2,320]{3,0,2,1:T(2,128)(2,1)}), bf16[2,80,2,320]{3,0,2,1:T(2,128)(2,1)}, u32[]{:S(2)}, u32[]{:S(2)}) async-start(bf16[2,80,2,320]{3,0,2,1:T(2,128)(2,1)} %copy.81), calls=%async_computation.2 | async-start | bytes 491520 | tf_op jit(solution)/shard_map/all_to_all | solution.py:92
  149.9 6.9 %fusion.85 = f32[6,768,320]{1,0,2:T(8,128)S(1)} fusion(f32[2,768,320]{1,2,0:T(8,128)} %get-tuple-element.529, s32[2]{0:T(128)S(1)} %copy-done.41), kind=kOutput, calls=%fused_computation.204 | convolution fusion | flops 35389452 | bytes 7864328 | tf_op jit(solution)/shard_map/ei,inc->enc/dot_general | solution.py:187
  156.9 5.4 %fusion.81 = f32[6,768,320]{1,0,2:T(8,128)S(1)} fusion(f32[2,768,320]{1,2,0:T(8,128)S(1)} %fusion.69, s32[2]{0:T(128)S(1)} %copy-done.40), kind=kOutput, calls=%fused_computation.200 | convolution fusion | flops 35389452 | bytes 7864328 | tf_op jit(solution)/shard_map/ei,inc->enc/dot_general | solution.py:187
  162.3 5.7 %fusion.83 = f32[6,768,320]{1,0,2:T(8,128)S(1)} fusion(f32[2,768,320]{1,2,0:T(8,128)S(1)} %copy-done.9, s32[2]{0:T(128)S(1)} %copy-done.39), kind=kOutput, calls=%fused_computation.202 | convolution fusion | flops 35389452 | bytes 7864328 | tf_op jit(solution)/shard_map/ei,inc->enc/dot_general | solution.py:187
  168.0 11.3 %fusion.153 = (bf16[6,768,320]{1,2,0:T(8,128)(2,1)}, f32[6,768,320]{1,2,0:T(8,128)}) fusion(f32[6,768,320]{1,0,2:T(8,128)S(1)} %fusion.81, f32[6,768,320]{1,0,2:T(8,128)S(1)} %fusion.83, f32[6,768,320]{1,0,2:T(8,128)S(1)} %fusion.85), kind=kLoop, calls=%fused_computation.319 | loop fusion | flops 4423680 | bytes 26542080 | tf_op jit(solution)/shard_map/convert.1
  179.4 3.0 fusion.155
  182.4 2.2 collective-permute-start.2
  184.6 4.4 %collective-permute-start.3 = (bf16[2,768,320]{1,2,0:T(8,128)(2,1)}, bf16[2,768,320]{1,2,0:T(8,128)(2,1)}, u32[]{:S(2)}, u32[]{:S(2)}) collective-permute-start(bf16[2,768,320]{1,2,0:T(8,128)(2,1)} %get-tuple-element.532), channel_id=1, source_target_pairs={{1,0},{2,1},{3,2},{4,3},{5,4},{6,5},{7,6},{8,7},{9,8},{10,9},{11,1... | collective-permute-start | bytes 2949128 | tf_op jit(solution)/shard_map/ppermute | solution.py:23
  189.0 1.1 copy.83
  190.3 1.0 multiply_reduce_fusion
  191.7 0.9 copy.84
  192.7 5.2 %all-to-all-start.3 = ((bf16[32,5,2,320]{3,2,1,0:T(2,128)(2,1)}), bf16[32,5,2,320]{3,2,1,0:T(2,128)(2,1)S(1)}, u32[]{:S(2)}, u32[]{:S(2)}) async-start(bf16[32,5,2,320]{3,2,1,0:T(2,128)(2,1)} %copy.84), calls=%async_computation.3 | async-start | bytes 491520 | tf_op jit(solution)/shard_map/all_to_all | solution.py:96
  198.6 13.6 %all-to-all-done.3 = bf16[32,5,2,320]{3,2,1,0:T(2,128)(2,1)S(1)} async-done(((bf16[32,5,2,320]{3,2,1,0:T(2,128)(2,1)}), bf16[32,5,2,320]{3,2,1,0:T(2,128)(2,1)S(1)}, u32[]{:S(2)}, u32[]{:S(2)}) %all-to-all-start.3) | async-done | bytes 204832 | tf_op jit(solution)/shard_map/all_to_all | solution.py:96
  212.4 3.6 %fusion.49 = (f32[320]{0:T(512)S(1)}, bf16[2,768,320]{1,2,0:T(8,128)(2,1)}) fusion(bf16[2,768,320]{1,2,0:T(8,128)(2,1)S(1)} %copy-done.10, bf16[2,768,320]{1,2,0:T(8,128)(2,1)} %collective-permute-done.3, bf16[2,768,320]{1,2,0:T(8,128)(2,1)S(1)} %collective-permute-done.2, f32[6,768,320]{1,2,0:T(8,128)} %get-tuple-element.442, ...), kind=kOutput, calls=%fused_computation.165 | convolution fusion | flops 162078400 | bytes 6595840 | tf_op jit(solution)/shard_map/jmrc,nmr->jnc/dot_general | solution.py:175
  216.0 23.6 %all-reduce = (f32[3,320]{1,0:T(4,128)}, f32[320]{0:T(512)}) all-reduce(f32[3,320]{1,0:T(4,128)S(1)} %convolution_bitcast_fusion, f32[320]{0:T(512)S(1)} %get-tuple-element.533), channel_id=1, replica_groups=mesh['ens'=2,'lat'=16] {'lat'}, use_global_device_ids=true, to_apply=%region_12.14 | all-reduce | flops 1280 | bytes 10240 | tf_op jit(solution)/shard_map/psum | solution.py:209
  239.6 53.6 %all-reduce.3.cloned.1.call-done = f32[80,320]{1,0:T(8,128)} async-done(((f32[80,320]{1,0:T(8,128)}), f32[80,320]{1,0:T(8,128)}) %all-reduce.3.cloned.1.call-update) | async-done | bytes 102416 | tf_op jit(solution)/shard_map/psum | solution.py:209
  293.2 1.6 copy.179
  (383 shorter events, 13.7 us)
Async XLA Ops:
  7.2 17.8 %copy-start = (f32[3,32,3,3]{1,3,2,0:T(4,128)S(1)}, f32[3,32,3,3]{1,3,2,0:T(4,128)}, u32[]{:S(2)}) copy-start(f32[3,32,3,3]{1,3,2,0:T(4,128)} %param.15) | copy-start | bytes 10372
  9.0 16.9 %copy-start.8 = (bf16[2,768,320]{1,2,0:T(8,128)(2,1)}, bf16[2,768,320]{1,2,0:T(8,128)(2,1)S(1)}, u32[]{:S(2)}) copy-start(bf16[2,768,320]{1,2,0:T(8,128)(2,1)S(1)} %fusion.48) | copy-start | bytes 2949124
  9.1 13.8 %copy-start.43 = (s32[32,3]{0,1:T(4,128)S(1)}, s32[32,3]{0,1:T(4,128)}, u32[]{:S(2)}) copy-start(s32[32,3]{0,1:T(4,128)} %param.16) | copy-start | bytes 1156
  9.1 16.1 %copy-start.27 = (f32[3,320]{1,0:T(4,128)S(1)}, f32[3,320]{1,0:T(4,128)}, u32[]{:S(2)}) copy-start(f32[3,320]{1,0:T(4,128)} %param.17) | copy-start | bytes 11524
  9.1 99.7 %collective-permute-start.1 = (bf16[2,768,320]{1,2,0:T(8,128)(2,1)S(1)}, bf16[2,768,320]{1,2,0:T(8,128)(2,1)S(1)}, u32[]{:S(2)}, u32[]{:S(2)}) collective-permute-start(bf16[2,768,320]{1,2,0:T(8,128)(2,1)S(1)} %fusion.48), channel_id=1, source_target_pairs={{1,0},{2,1},{3,2},{4,3},{5,4},{6,5},{7,6},{8,7},{9,8},{10,9},{11,1... | collective-permute-start | bytes 2949128 | tf_op jit(solution)/shard_map/ppermute | solution.py:15
  12.0 97.8 %collective-permute-start = (bf16[2,768,320]{1,2,0:T(8,128)(2,1)S(1)}, bf16[2,768,320]{1,2,0:T(8,128)(2,1)}, u32[]{:S(2)}, u32[]{:S(2)}) collective-permute-start(bf16[2,768,320]{1,2,0:T(8,128)(2,1)S(1)} %fusion.48), channel_id=1, source_target_pairs={{0,1},{1,2},{2,3},{3,4},{4,5},{5,6},{6,7},{7,8},{8,9},{9,10},{10,1... | collective-permute-start | bytes 2949128 | tf_op jit(solution)/shard_map/ppermute | solution.py:14
  16.3 74.9 %all-to-all-start = ((bf16[2,80,2,320]{3,0,2,1:T(2,128)(2,1)}), bf16[2,80,2,320]{3,0,2,1:T(2,128)(2,1)S(1)}, u32[]{:S(2)}, u32[]{:S(2)}) async-start(bf16[2,80,2,320]{3,0,2,1:T(2,128)(2,1)} %copy.75), calls=%async_computation | async-start | bytes 491520 | tf_op jit(solution)/shard_map/all_to_all | solution.py:92
  25.2 0.8 copy-start.21
  90.4 2.7 copy-start.16
  91.1 2.3 copy-start.37
  91.6 9.4 %copy-start.24 = (f32[2,1,1,320]{3,2,1,0:T(1,128)S(1)}, f32[2,1,1,320]{3,2,1,0:T(1,128)}, u32[]{:S(2)}) copy-start(f32[2,1,1,320]{3,2,1,0:T(1,128)} %get-tuple-element.551) | copy-start | bytes 7684
  91.6 9.4 %copy-start.42 = (s32[2]{0:T(128)S(1)}, s32[2]{0:T(128)}, u32[]{:S(2)}) copy-start(s32[2]{0:T(128)} %get-tuple-element.566) | copy-start | bytes 28
  91.6 10.0 %copy-start.25 = (f32[2,1,1,320]{3,2,1,0:T(1,128)S(1)}, f32[2,1,1,320]{3,2,1,0:T(1,128)}, u32[]{:S(2)}) copy-start(f32[2,1,1,320]{3,2,1,0:T(1,128)} %get-tuple-element.558) | copy-start | bytes 7684
  91.6 10.0 %copy-start.26 = (f32[2,1,1,320]{3,2,1,0:T(1,128)S(1)}, f32[2,1,1,320]{3,2,1,0:T(1,128)}, u32[]{:S(2)}) copy-start(f32[2,1,1,320]{3,2,1,0:T(1,128)} %get-tuple-element.559) | copy-start | bytes 7684
  92.1 1.0 copy-start.2
  94.2 13.7 %all-to-all-start.1 = ((bf16[32,5,2,320]{3,2,1,0:T(2,128)(2,1)}), bf16[32,5,2,320]{3,2,1,0:T(2,128)(2,1)S(1)}, u32[]{:S(2)}, u32[]{:S(2)}) async-start(bf16[32,5,2,320]{3,2,1,0:T(2,128)(2,1)} %copy.78), calls=%async_computation.1 | async-start | bytes 491520 | tf_op jit(solution)/shard_map/all_to_all | solution.py:96
  108.8 0.9 copy-start.11
  117.0 2.7 copy-start.4
  117.0 3.5 %copy-start.6 = (bf16[2,768,320]{1,2,0:T(8,128)(2,1)}, bf16[2,768,320]{1,2,0:T(8,128)(2,1)S(1)}, u32[]{:S(2)}) copy-start(bf16[2,768,320]{1,2,0:T(8,128)(2,1)S(1)} %get-tuple-element.572) | copy-start | bytes 2949124
  123.9 2.2 copy-start.14
  123.9 2.2 copy-start.15
  125.4 1.0 copy-start.18
  125.5 1.1 copy-start.19
  125.5 1.1 copy-start.20
  125.6 1.3 copy-start.5
  125.6 1.6 copy-start.7
  125.6 1.9 copy-start.12
  125.6 2.1 copy-start.13
  125.6 2.1 copy-start.23
  125.6 2.1 copy-start.44
  139.1 10.8 %copy-start.41 = (s32[2]{0:T(128)S(1)}, s32[2]{0:T(128)}, u32[]{:S(2)}) copy-start(s32[2]{0:T(128)} %get-tuple-element.560) | copy-start | bytes 28
  143.4 45.6 %all-to-all-start.2 = ((bf16[2,80,2,320]{3,0,2,1:T(2,128)(2,1)}), bf16[2,80,2,320]{3,0,2,1:T(2,128)(2,1)}, u32[]{:S(2)}, u32[]{:S(2)}) async-start(bf16[2,80,2,320]{3,0,2,1:T(2,128)(2,1)} %copy.81), calls=%async_computation.2 | async-start | bytes 491520 | tf_op jit(solution)/shard_map/all_to_all | solution.py:92
  149.9 7.0 %copy-start.40 = (s32[2]{0:T(128)S(1)}, s32[2]{0:T(128)}, u32[]{:S(2)}) copy-start(s32[2]{0:T(128)} %get-tuple-element.561) | copy-start | bytes 28
  156.9 5.5 %copy-start.9 = (f32[2,768,320]{1,2,0:T(8,128)S(1)}, f32[2,768,320]{1,2,0:T(8,128)}, u32[]{:S(2)}) copy-start(f32[2,768,320]{1,2,0:T(8,128)} %get-tuple-element.530) | copy-start | bytes 5898244
  156.9 5.5 %copy-start.39 = (s32[2]{0:T(128)S(1)}, s32[2]{0:T(128)}, u32[]{:S(2)}) copy-start(s32[2]{0:T(128)} %get-tuple-element.562) | copy-start | bytes 28
  179.4 10.9 %copy-start.3 = (f32[5,80,2,320]{3,1,2,0:T(8,128)S(1)}, f32[5,80,2,320]{3,1,2,0:T(8,128)}, u32[]{:S(2)}) copy-start(f32[5,80,2,320]{3,1,2,0:T(8,128)} %copy-done.2) | copy-start | bytes 3072004
  182.4 9.1 %copy-start.17 = (f32[80,320]{1,0:T(8,128)S(1)}, f32[80,320]{1,0:T(8,128)}, u32[]{:S(2)}) copy-start(f32[80,320]{1,0:T(8,128)} %param.18) | copy-start | bytes 307204
  182.4 9.1 %copy-start.38 = (f32[32]{0:T(128)S(1)}, f32[32]{0:T(128)}, u32[]{:S(2)}) copy-start(f32[32]{0:T(128)} %copy-done.37) | copy-start | bytes 388
  182.4 30.0 %collective-permute-start.2 = (bf16[2,768,320]{1,2,0:T(8,128)(2,1)}, bf16[2,768,320]{1,2,0:T(8,128)(2,1)S(1)}, u32[]{:S(2)}, u32[]{:S(2)}) collective-permute-start(bf16[2,768,320]{1,2,0:T(8,128)(2,1)} %get-tuple-element.531), channel_id=1, source_target_pairs={{0,1},{1,2},{2,3},{3,4},{4,5},{5,6},{6,7},{7,8},{8,9},{9,10},{10,1... | collective-permute-start | bytes 2949128 | tf_op jit(solution)/shard_map/ppermute | solution.py:23
  184.6 27.8 %collective-permute-start.3 = (bf16[2,768,320]{1,2,0:T(8,128)(2,1)}, bf16[2,768,320]{1,2,0:T(8,128)(2,1)}, u32[]{:S(2)}, u32[]{:S(2)}) collective-permute-start(bf16[2,768,320]{1,2,0:T(8,128)(2,1)} %get-tuple-element.532), channel_id=1, source_target_pairs={{1,0},{2,1},{3,2},{4,3},{5,4},{6,5},{7,6},{8,7},{9,8},{10,9},{11,1... | collective-permute-start | bytes 2949128 | tf_op jit(solution)/shard_map/ppermute | solution.py:23
  191.3 6.6 %copy-start.34 = (f32[2,320]{1,0:T(2,128)S(1)}, f32[2,320]{1,0:T(2,128)}, u32[]{:S(2)}) copy-start(f32[2,320]{1,0:T(2,128)} %get-tuple-element.392) | copy-start | bytes 7684
  191.3 6.6 %copy-start.35 = (f32[2,320]{1,0:T(2,128)S(1)}, f32[2,320]{1,0:T(2,128)}, u32[]{:S(2)}) copy-start(f32[2,320]{1,0:T(2,128)} %get-tuple-element.393) | copy-start | bytes 7684
  191.3 6.6 %copy-start.36 = (f32[2,320]{1,0:T(2,128)S(1)}, f32[2,320]{1,0:T(2,128)}, u32[]{:S(2)}) copy-start(f32[2,320]{1,0:T(2,128)} %get-tuple-element.394) | copy-start | bytes 7684
  191.3 6.6 %copy-start.31 = (f32[2,320]{1,0:T(2,128)S(1)}, f32[2,320]{1,0:T(2,128)}, u32[]{:S(2)}) copy-start(f32[2,320]{1,0:T(2,128)} %get-tuple-element.395) | copy-start | bytes 7684
  191.3 6.6 %copy-start.32 = (f32[2,320]{1,0:T(2,128)S(1)}, f32[2,320]{1,0:T(2,128)}, u32[]{:S(2)}) copy-start(f32[2,320]{1,0:T(2,128)} %get-tuple-element.396) | copy-start | bytes 7684
  191.3 6.6 %copy-start.33 = (f32[2,320]{1,0:T(2,128)S(1)}, f32[2,320]{1,0:T(2,128)}, u32[]{:S(2)}) copy-start(f32[2,320]{1,0:T(2,128)} %get-tuple-element.397) | copy-start | bytes 7684
  191.4 6.6 %copy-start.28 = (f32[2,320]{1,0:T(2,128)S(1)}, f32[2,320]{1,0:T(2,128)}, u32[]{:S(2)}) copy-start(f32[2,320]{1,0:T(2,128)} %get-tuple-element.398) | copy-start | bytes 7684
  191.4 6.6 %copy-start.29 = (f32[2,320]{1,0:T(2,128)S(1)}, f32[2,320]{1,0:T(2,128)}, u32[]{:S(2)}) copy-start(f32[2,320]{1,0:T(2,128)} %get-tuple-element.399) | copy-start | bytes 7684
  191.4 6.6 %copy-start.30 = (f32[2,320]{1,0:T(2,128)S(1)}, f32[2,320]{1,0:T(2,128)}, u32[]{:S(2)}) copy-start(f32[2,320]{1,0:T(2,128)} %get-tuple-element.400) | copy-start | bytes 7684
  191.4 6.7 %copy-start.22 = (f32[3,2,3,3]{0,3,2,1:T(4,128)S(1)}, f32[3,2,3,3]{0,3,2,1:T(4,128)}, u32[]{:S(2)}) copy-start(f32[3,2,3,3]{0,3,2,1:T(4,128)} %copy-done.21) | copy-start | bytes 652
  191.4 21.0 %copy-start.10 = (bf16[2,768,320]{1,2,0:T(8,128)(2,1)S(1)}, bf16[2,768,320]{1,2,0:T(8,128)(2,1)}, u32[]{:S(2)}) copy-start(bf16[2,768,320]{1,2,0:T(8,128)(2,1)} %param.13) | copy-start | bytes 2949124
  192.7 19.5 %all-to-all-start.3 = ((bf16[32,5,2,320]{3,2,1,0:T(2,128)(2,1)}), bf16[32,5,2,320]{3,2,1,0:T(2,128)(2,1)S(1)}, u32[]{:S(2)}, u32[]{:S(2)}) async-start(bf16[32,5,2,320]{3,2,1,0:T(2,128)(2,1)} %copy.84), calls=%async_computation.3 | async-start | bytes 491520 | tf_op jit(solution)/shard_map/all_to_all | solution.py:96
  197.8 95.3 %all-reduce.3.cloned.1.call-start = ((), (), s32[]{:S(2)}) async-start(), calls=%async_computation.4 | async-start | bytes 245760 | tf_op jit(solution)/shard_map/psum | solution.py:209
  212.3 82.4 %copy-start.1 = (f32[3,32,3,3]{1,3,2,0:T(4,128)S(1)}, f32[3,32,3,3]{1,3,2,0:T(4,128)}, u32[]{:S(2)}) copy-start(f32[3,32,3,3]{1,3,2,0:T(4,128)} %param.15) | copy-start | bytes 10372
Sparse Core Ops, SparseCore 0:
  202.7 90.4 all-reduce.2
where the time goes:
time: 308 us; the launch traced here: 302 us
  waiting for transfers between devices  73.2 us (24%)
  loops' own time  51.3 us (17%)
  other arithmetic  36.6 us (12%)
  starting transfers between devices  35.9 us (12%)
  matrix products  34.1 us (11%)
  local copies, waits for them, and re-layouts  32 us (10%)
  blocking collectives  23.6 us (8%)
  between operations  15.3 us (5%)
    psum x1, waiting for transfers between devices, body(): lax.psum((basis_part, gain_part, scale_part), 'lat')  53.6 us
    another operation x1, loops' own time, legendre_table(): lax.scan(advance, (blank_rows, blank_rows), jnp.arange(degree_count, dtyp...  51.3 us
    psum x1, blocking collectives, body(): lax.psum((basis_part, gain_part, scale_part), 'lat')  23.6 us
    all_to_all x2, waiting for transfers between devices, to_band(): lax.all_to_all(values_pencil, 'lat', split_axis=0, concat_axis=1, tiled=T...  19.3 us
    dot_general x3, matrix products, body(): jnp.einsum('ei,inc->enc', onehot, spread, precision=highest)  18 us
    all_to_all x2, starting transfers between devices, to_pencil(): lax.all_to_all(values_band, 'lat', split_axis=1, concat_axis=0, tiled=True)  13 us
    all_to_all x2, starting transfers between devices, to_band(): lax.all_to_all(values_pencil, 'lat', split_axis=0, concat_axis=1, tiled=T...  11.5 us
    another operation x1, other arithmetic  11.3 us
  transfers between devices with their start and end apart: 9, of which 3 were waited for; matrix products, arithmetic and copies ran while one was open for 21% of the time, Pallas kernels for 0%

commit v1 on v0

v1 whole, which is shorter than its diff:
```python
import functools
import math

import jax
import jax.numpy as jnp
import numpy as np
from jax import lax
from jax.experimental import pallas as pl
from jax.experimental.pallas import tpu as pltpu
from jax.sharding import PartitionSpec as P

F32, BF16 = jnp.float32, jnp.bfloat16
MESH = pl.DeviceIdType.MESH
SLOTS = 16


def legendre_numpy(modes, lats, degrees):
    u = np.pi * (np.arange(lats) + 0.5) / lats
    order = np.arange(modes, dtype=np.float64)[:, None]
    k = np.arange(1, modes + 1, dtype=np.float64)
    steps = np.concatenate([[0.0], np.cumsum(0.5 * np.log((2 * k + 1) / (2 * k)))])[:modes]
    start = np.exp(
        0.5 * np.log(1 / (4 * np.pi)) + steps[:, None] + order * np.log(np.sin(u))[None, :]
    )
    out = np.zeros((modes, degrees, lats))
    one = np.zeros((modes, lats))
    two = np.zeros((modes, lats))
    for l in range(degrees):
        a = np.sqrt((4.0 * l * l - 1 if l else 0.0) / np.maximum(l * l - order**2, 1.0))
        b = np.sqrt(
            np.maximum((l - 1.0) ** 2 - order**2, 0.0) / np.maximum(4 * (l - 1.0) ** 2 - 1, 1.0)
        )
        general = a * (np.cos(u)[None, :] * one - b * two)
        now = np.where(l < order, 0.0, np.where(l == order, start, general))
        out[:, l] = now
        one, two = now, one
    weight = np.pi / lats * np.sin(u)
    return (out * weight).astype(jnp.bfloat16), out.astype(jnp.bfloat16)


def fourier_numpy(lons, devices, each):
    modes = devices * each
    n = np.arange(lons)
    m = np.arange(modes)
    p = 2 * np.pi * ((n[None, :] * m[:, None]) % lons) / lons
    pair = np.stack([np.cos(p), -np.sin(p)], axis=1)
    forward = pair * (2 * np.pi / lons)
    inverse = pair * np.where(m == 0, 1.0, 2.0)[:, None, None]

    def padded(table):
        out = np.zeros((devices, SLOTS, lons))
        out[:, : 2 * each] = table.reshape(devices, 2 * each, lons)
        return out.reshape(devices * SLOTS, lons).astype(jnp.bfloat16)

    return padded(forward), padded(inverse)


def dot(a, b):
    return lax.dot_general(a, b, (((1,), (0,)), ((), ())), preferred_element_type=F32)


def dot_turned(a, b):
    return lax.dot_general(a, b, (((0,), (0,)), ((), ())), preferred_element_type=F32)


def kernel(
    dims,
    filt,
    rows,
    state,
    noise,
    cot,
    scale,
    weight,
    gain,
    fwd,
    fwd_t,
    inv,
    inv_t,
    pick,
    pick_t,
    table,
    out,
    basis_out,
    gain_out,
    scale_out,
    pad,
    gpad,
    ls,
    ysc,
    cf,
    ef,
    coef,
    gacc,
    pencil,
    sorted_rows,
    send,
    recv,
    gain_in,
    gain_sum,
    small,
    small_in,
    a2a_send,
    a2a_recv,
    halo_send,
    halo_recv,
    gain_send,
    gain_recv,
    gat_send,
    gat_recv,
    small_send,
    small_recv,
):
    devices, each, lons, chans, degrees, lats = dims
    span = 2
    me = lax.axis_index("lat")
    first = me * span
    chunk, wide = 32, 128
    groups = chunk // 8
    reducers = degrees // 8

    def peer_of(off):
        return lax.rem(me + off, devices)

    def source_of(off):
        return lax.rem(me - off + devices, devices)

    barrier = pltpu.get_barrier_semaphore()

    def greet(off, z):
        pl.semaphore_signal(barrier, inc=1, device_id={"lat": peer_of(off)}, device_id_type=MESH)
        return z

    lax.fori_loop(1, devices, greet, 0)

    def block_copy(phase, off, peer):
        return pltpu.make_async_remote_copy(
            src_ref=send.at[phase, peer],
            dst_ref=recv.at[phase, me],
            send_sem=a2a_send.at[phase, off],
            recv_sem=a2a_recv.at[phase, off],
            device_id={"lat": peer},
            device_id_type=MESH,
        )

    def exchange(phase):
        def go(off, z):
            block_copy(phase, off, peer_of(off)).start()
            return z

        lax.fori_loop(1, devices, go, 0)
        recv[phase, me] = send[phase, me]

    def arrive(phase):
        def take(off, z):
            block_copy(phase, off, peer_of(off)).wait_recv()
            return z

        lax.fori_loop(1, devices, take, 0)

    def halo_copies(buffer, phase):
        up = pltpu.make_async_remote_copy(
            src_ref=buffer.at[pl.ds(2, 2)],
            dst_ref=buffer.at[pl.ds(4, 2)],
            send_sem=halo_send.at[phase, 0],
            recv_sem=halo_recv.at[phase, 0],
            device_id={"lat": lax.rem(me + devices - 1, devices)},
            device_id_type=MESH,
        )
        down = pltpu.make_async_remote_copy(
            src_ref=buffer.at[pl.ds(2, 2)],
            dst_ref=buffer.at[pl.ds(0, 2)],
            send_sem=halo_send.at[phase, 1],
            recv_sem=halo_recv.at[phase, 1],
            device_id={"lat": lax.rem(me + 1, devices)},
            device_id_type=MESH,
        )
        return up, down

    def halo_start(buffer, phase):
        up, down = halo_copies(buffer, phase)

        @pl.when(me > 0)
        def _():
            up.start()

        @pl.when(me < devices - 1)
        def _():
            down.start()

    def halo_arrive(buffer, phase):
        up, down = halo_copies(buffer, phase)

        @pl.when(me < devices - 1)
        def _():
            up.wait_recv()

        @pl.when(me > 0)
        def _():
            down.wait_recv()

    def halo_sent(buffer, phase):
        up, down = halo_copies(buffer, phase)

        @pl.when(me > 0)
        def _():
            up.wait_send()

        @pl.when(me < devices - 1)
        def _():
            down.wait_send()

    def at(c, size=chunk):
        return pl.ds(pl.multiple_of(c * size, size), size)

    def around(c, shift):
        return pl.ds(pl.multiple_of(c * chunk + shift, 8), chunk + 8)

    def before(x):
        return pltpu.roll(x, 1, 0)[8:]

    def after(x):
        return pltpu.roll(x, chunk + 7, 0)[:chunk]

    def tall(x):
        return x.reshape(groups, 8, chans)

    sc = scale[...]
    for j in range(span):

        def noisy(c, z):
            pad[2 + j, at(c)] = (
                state[j, at(c)].astype(F32) + sc * noise[j, at(c)].astype(F32)
            ).astype(BF16)
            return z

        lax.fori_loop(0, lons // chunk, noisy, 0)
        send[0, :, j] = (
            dot(fwd[...], pad[2 + j]).astype(BF16).reshape(devices, SLOTS, chans)
        )

    pl.semaphore_wait(barrier, devices - 1)
    exchange(0)
    halo_start(pad, 0)

    @pl.when(me == 0)
    def _():
        pad[0:2] = jnp.zeros((2, lons, chans), BF16)
        gpad[0:2] = jnp.zeros((2, lons, chans), BF16)

    @pl.when(me == devices - 1)
    def _():
        pad[4:6] = jnp.zeros((2, lons, chans), BF16)
        gpad[4:6] = jnp.zeros((2, lons, chans), BF16)

    def filter_row(row, t, s):
        total = jnp.zeros((1, chans), F32)
        for k in range(3):
            total = total + filt[((k * lats + row) * 3 + t) * 3 + s] * weight[k : k + 1, :]
        return total

    for i in range(span):
        for t in range(3):
            for s in range(3):
                cf[i * 9 + t * 3 + s] = jnp.broadcast_to(
                    filter_row(first + i, t, s), (8, chans)
                )
    for q in range(span):
        for e in range(5):
            row = lax.rem(first - 2 + q + e + lats, lats)
            taps = (2,) if e < 2 else ((0,) if e > 2 else (0, 1, 2))
            for s in range(3):
                total = jnp.zeros((1, chans), F32)
                for t in taps:
                    hit = jnp.where(rows[row * 3 + t] == first + q, 1.0, 0.0).astype(F32)
                    total = total + hit * filter_row(row, t, s)
                ef[q * 15 + e * 3 + s] = jnp.broadcast_to(total, (8, chans))

    arrive(0)

    def gather_rows(phase):
        block = recv[phase].reshape(devices * span * SLOTS, chans)
        pieces = max(devices // 16, 1)
        size = 2 * each * lats // pieces
        for piece in range(pieces):
            part = pl.ds(piece * size, size)
            pencil[part] = dot(pick[part], block).astype(BF16)

    def scatter_rows(phase):
        pieces = max(devices // 16, 1)
        size = devices // pieces
        for piece in range(pieces):
            part = pl.ds(piece * size * span * SLOTS, size * span * SLOTS)
            send[phase, pl.ds(piece * size, size)] = (
                dot(pick_t[part], sorted_rows[...]).astype(BF16).reshape(size, span, SLOTS, chans)
            )

    gather_rows(0)
    gains = gain[...]

    def analyse(m, z):
        for r in range(2):
            cm = dot(table[0, at(m, degrees)], pencil[at(2 * m + r, lats)])
            coef[2 * m + r] = cm
            sorted_rows[at(2 * m + r, lats)] = dot_turned(
                table[1, at(m, degrees)], (gains * cm).astype(BF16)
            ).astype(BF16)
        return z

    lax.fori_loop(0, each, analyse, 0)
    scatter_rows(1)
    exchange(1)

    halo_arrive(pad, 0)

    def picked(i, t, c):
        slot = jnp.clip(rows[(first + i) * 3 + t] - first + 2, 0, 5)
        return pad[slot, at(c)].astype(F32)

    for i in range(span):

        def taps_of(c, z):
            y = [None, None, None]
            for t in range(3):
                x = tall(picked(i, t, c))
                for s in range(3):
                    term = cf[i * 9 + t * 3 + s][None] * x
                    y[s] = term if t == 0 else y[s] + term
            here = pl.ds(pl.multiple_of(8 + c * chunk, 8), chunk)
            ysc[0, here] = y[0].reshape(chunk, chans)
            ysc[1, here] = y[2].reshape(chunk, chans)
            ls[i, at(c)] = y[1].reshape(chunk, chans)
            return z

        lax.fori_loop(0, lons // chunk, taps_of, 0)
        ysc[0, 7:8] = ysc[0, lons + 7 : lons + 8]
        ysc[1, lons + 8 : lons + 9] = ysc[1, 8:9]

        def join(c, z):
            ls[i, at(c)] += (
                before(ysc[0, around(c, 0)]) + after(ysc[1, around(c, 8)])
            )
            return z

        lax.fori_loop(0, lons // chunk, join, 0)

    arrive(1)

    root = math.sqrt(2.0 / math.pi)
    for j in range(span):
        returned = recv[1, :, j].reshape(devices * SLOTS, chans)

        def activate(c, z):
            v = ls[j, at(c, wide)] + dot(inv_t[at(c, wide)], returned)
            square = v * v
            th = jnp.tanh(root * v * (1.0 + 0.044715 * square))
            slope = 0.5 * (1.0 + th) + 0.5 * v * (1.0 - th * th) * root * (
                1.0 + 3 * 0.044715 * square
            )
            gpad[2 + j, at(c, wide)] = (cot[j, at(c, wide)].astype(F32) * slope).astype(BF16)
            return z

        lax.fori_loop(0, lons // wide, activate, 0)
        send[2, :, j] = (
            dot(inv[...], gpad[2 + j]).astype(BF16).reshape(devices, SLOTS, chans)
        )
    exchange(2)
    halo_start(gpad, 1)

    basis = [jnp.zeros((1, chans), F32) for _ in range(3)]
    for i in range(span):

        def widen(c, z):
            ysc[0, pl.ds(pl.multiple_of(8 + c * chunk, 8), chunk)] = gpad[2 + i, at(c)].astype(F32)
            return z

        lax.fori_loop(0, lons // chunk, widen, 0)
        ysc[0, 7:8] = ysc[0, lons + 7 : lons + 8]
        ysc[0, lons + 8 : lons + 9] = ysc[0, 8:9]

        def correlate(c, sums):
            g = [
                tall(after(ysc[0, around(c, 8)])),
                tall(ysc[0, pl.ds(pl.multiple_of(8 + c * chunk, 8), chunk)]),
                tall(before(ysc[0, around(c, 0)])),
            ]
            new = []
            for t in range(3):
                x = tall(picked(i, t, c))
                for s in range(3):
                    new.append(sums[t * 3 + s] + jnp.sum(g[s] * x, axis=0))
            return tuple(new)

        sums = lax.fori_loop(
            0, lons // chunk, correlate, tuple(jnp.zeros((8, chans), F32) for _ in range(9))
        )
        for t in range(3):
            for s in range(3):
                total = jnp.sum(sums[t * 3 + s], axis=0, keepdims=True)
                for k in range(3):
                    basis[k] = (
                        basis[k] + filt[((k * lats + first + i) * 3 + t) * 3 + s] * total
                    )
    small[...] = jnp.zeros((8, chans), F32)
    for k in range(3):
        small[k : k + 1] = basis[k]

    arrive(2)
    gather_rows(2)
    gacc[...] = jnp.zeros((degrees, chans), F32)

    def analyse_back(m, z):
        for r in range(2):
            gm = dot(table[1, at(m, degrees)], pencil[at(2 * m + r, lats)])
            gacc[...] += coef[2 * m + r] * gm
            sorted_rows[at(2 * m + r, lats)] = dot_turned(
                table[0, at(m, degrees)], (gains * gm).astype(BF16)
            ).astype(BF16)
        return z

    lax.fori_loop(0, each, analyse_back, 0)
    scatter_rows(3)
    exchange(3)

    def gain_copy(off, peer):
        return pltpu.make_async_remote_copy(
            src_ref=gacc.at[pl.ds(pl.multiple_of(lax.rem(peer, reducers) * 8, 8), 8)],
            dst_ref=gain_in.at[me],
            send_sem=gain_send.at[off],
            recv_sem=gain_recv.at[off],
            device_id={"lat": peer},
            device_id_type=MESH,
        )

    def total_copy(off, peer):
        return pltpu.make_async_remote_copy(
            src_ref=gain_sum.at[me],
            dst_ref=gain_sum.at[me],
            send_sem=gat_send.at[off],
            recv_sem=gat_recv.at[off],
            device_id={"lat": peer},
            device_id_type=MESH,
        )

    def gain_go(off, z):
        peer = peer_of(off)

        @pl.when(peer < reducers)
        def _():
            gain_copy(off, peer).start()

        return z

    lax.fori_loop(1, devices, gain_go, 0)

    halo_arrive(gpad, 1)
    for q in range(span):

        def spread_of(c, z):
            y = [None, None, None]
            for e in range(5):
                x = tall(gpad[q + e, at(c)].astype(F32))
                for s in range(3):
                    term = ef[q * 15 + e * 3 + s][None] * x
                    y[s] = term if e == 0 else y[s] + term
            here = pl.ds(pl.multiple_of(8 + c * chunk, 8), chunk)
            ysc[0, here] = y[2].reshape(chunk, chans)
            ysc[1, here] = y[0].reshape(chunk, chans)
            ls[q, at(c)] = y[1].reshape(chunk, chans)
            return z

        lax.fori_loop(0, lons // chunk, spread_of, 0)
        ysc[0, 7:8] = ysc[0, lons + 7 : lons + 8]
        ysc[1, lons + 8 : lons + 9] = ysc[1, 8:9]

        def join_back(c, z):
            ls[q, at(c)] += (
                before(ysc[0, around(c, 0)]) + after(ysc[1, around(c, 8)])
            )
            return z

        lax.fori_loop(0, lons // chunk, join_back, 0)

    @pl.when(me < reducers)
    def _():
        gain_in[me] = gacc[pl.ds(pl.multiple_of(lax.rem(me, reducers) * 8, 8), 8)]

        def take(off, z):
            gain_copy(off, peer_of(off)).wait_recv()
            return z

        lax.fori_loop(1, devices, take, 0)
        gain_sum[me] = jnp.sum(gain_in[...], axis=0)

        def give(off, z):
            total_copy(off, peer_of(off)).start()
            return z

        lax.fori_loop(1, devices, give, 0)

    arrive(3)
    accs = jnp.zeros((8, chans), F32)
    for j in range(span):
        back = recv[3, :, j].reshape(devices * SLOTS, chans)

        def finish(c, acc):
            total = ls[j, at(c, wide)] + dot(fwd_t[at(c, wide)], back)
            out[j, at(c, wide)] = total.astype(BF16)
            prod = total * noise[j, at(c, wide)].astype(F32)
            return acc + jnp.sum(prod.reshape(wide // 8, 8, chans), axis=0)

        accs = lax.fori_loop(0, lons // wide, finish, accs)
    small[3:4] = jnp.sum(accs, axis=0, keepdims=True)

    def small_copy(off, peer):
        return pltpu.make_async_remote_copy(
            src_ref=small,
            dst_ref=small_in.at[me],
            send_sem=small_send.at[off],
            recv_sem=small_recv.at[off],
            device_id={"lat": peer},
            device_id_type=MESH,
        )

    def small_go(off, z):
        small_copy(off, peer_of(off)).start()
        return z

    lax.fori_loop(1, devices, small_go, 0)
    small_in[me] = small[...]

    def gain_take(off, z):
        @pl.when(source_of(off) < reducers)
        def _():
            total_copy(off, peer_of(off)).wait_recv()

        return z

    lax.fori_loop(1, devices, gain_take, 0)
    gain_out[...] = gain_sum[0:reducers].reshape(degrees, chans)

    def small_take(off, z):
        small_copy(off, peer_of(off)).wait_recv()
        return z

    lax.fori_loop(1, devices, small_take, 0)
    sums = jnp.sum(small_in[...], axis=0)
    basis_out[...] = sums[0:3]
    scale_out[...] = sums[3:4]

    def sent(off, z):
        peer = peer_of(off)
        for phase in range(4):
            block_copy(phase, off, peer).wait_send()
        small_copy(off, peer).wait_send()

        @pl.when(peer < reducers)
        def _():
            gain_copy(off, peer).wait_send()

        @pl.when(me < reducers)
        def _():
            total_copy(off, peer).wait_send()

        return z

    lax.fori_loop(1, devices, sent, 0)
    halo_sent(pad, 0)
    halo_sent(gpad, 1)


def body(state, noise, scale, filt, rows, weight, gain, cot):
    devices = lax.axis_size("lat")
    span, lons, chans = state.shape
    degrees = gain.shape[0]
    lats = span * devices
    each = degrees // devices
    analysis, synthesis = legendre_numpy(degrees, lats, degrees)
    forward, inverse = fourier_numpy(lons, devices, each)

    tables = np.stack(
        [t.reshape(devices, each * degrees, lats) for t in (analysis, synthesis)], axis=1
    )
    table = lax.dynamic_index_in_dim(tables, lax.axis_index("lat"), 0, keepdims=False)
    pick = np.zeros((2 * each, lats, lats, SLOTS), jnp.bfloat16)
    for slot in range(2 * each):
        pick[slot, np.arange(lats), np.arange(lats), slot] = 1
    pick = pick.reshape(2 * each * lats, lats * SLOTS)
    vmem = pl.BlockSpec(memory_space=pltpu.VMEM)
    smem = pl.BlockSpec(memory_space=pltpu.SMEM)
    dma = pltpu.SemaphoreType.DMA
    out, basis, gains, scales = pl.pallas_call(
        functools.partial(kernel, (devices, each, lons, chans, degrees, lats)),
        out_shape=(
            jax.ShapeDtypeStruct((span, lons, chans), BF16),
            jax.ShapeDtypeStruct((3, chans), F32),
            jax.ShapeDtypeStruct((degrees, chans), F32),
            jax.ShapeDtypeStruct((1, chans), F32),
        ),
        in_specs=[smem, smem] + [vmem] * 13,
        out_specs=(vmem,) * 4,
        scratch_shapes=[
            pltpu.VMEM((6, lons, chans), BF16),
            pltpu.VMEM((6, lons, chans), BF16),
            pltpu.VMEM((2, lons, chans), F32),
            pltpu.VMEM((2, lons + 16, chans), F32),
            pltpu.VMEM((18, 8, chans), F32),
            pltpu.VMEM((30, 8, chans), F32),
            pltpu.VMEM((2 * each, degrees, chans), F32),
            pltpu.VMEM((degrees, chans), F32),
            pltpu.VMEM((2 * each * lats, chans), BF16),
            pltpu.VMEM((2 * each * lats, chans), BF16),
            pltpu.VMEM((4, devices, span, SLOTS, chans), BF16),
            pltpu.VMEM((4, devices, span, SLOTS, chans), BF16),
            pltpu.VMEM((devices, 8, chans), F32),
            pltpu.VMEM((devices, 8, chans), F32),
            pltpu.VMEM((8, chans), F32),
            pltpu.VMEM((devices, 8, chans), F32),
            dma((4, devices)),
            dma((4, devices)),
            dma((2, 2)),
            dma((2, 2)),
            dma((devices,)),
            dma((devices,)),
            dma((devices,)),
            dma((devices,)),
            dma((devices,)),
            dma((devices,)),
        ],
        compiler_params=pltpu.CompilerParams(
            collective_id=0, has_side_effects=True, vmem_limit_bytes=60 * 1024 * 1024
        ),
        name="block_and_gradient",
    )(
        filt.reshape(-1),
        rows.reshape(-1),
        state,
        noise,
        cot,
        scale.reshape(1, chans),
        weight,
        gain,
        forward,
        np.ascontiguousarray(forward.T),
        inverse,
        np.ascontiguousarray(inverse.T),
        pick,
        np.ascontiguousarray(pick.T),
        table,
    )
    return out, basis, gains, scales.reshape(chans)


def solution(mesh):
    field = P(("ens", "lat"), None, None)
    return jax.shard_map(
        body,
        mesh=mesh,
        in_specs=(field, field, P(), P(), P(), P(), P(), field),
        out_specs=(field, P("ens", None), P("ens", None), P("ens")),
        check_vma=False,
    )
```

time: 308 us -> 115 us (0.37)
  the two profiles are of different devices: /device:TPU:8 before, /device:TPU:0 now
where the time goes in v1:
time: 115 us
  Pallas kernels  99 us (86%)
  local copies, waits for them, and re-layouts  14.8 us (13%)
    pallas_call x1, Pallas kernels, body(): pl.pallas_call(functools.partial(kernel, (devices, each, lons, chans, deg...  99 us
    unnamed x18, local copies, waits for them, and re-layouts  10.5 us

profile of v1, /device:TPU:0, one launch (start us, length us, event | category | flops | bytes accessed | tf_op | source)
XLA Modules:
  0.0 115.0 jit_solution(5238780238936414478)
XLA Ops:
  0.6 1.2 %reshape.22.scale = f32[1,320]{1,0:T(1,128)} reshape(f32[320]{0:T(512)} %param.17) | data formatting | bytes 2560 | tf_op jit(solution)/shard_map/reshape | solution.py:640
  1.9 0.8 copy.25
  2.6 0.6 reshape.21.rows
  3.3 0.9 copy.24
  4.1 0.8 reshape.20.filt
  4.9 1.6 %dynamic-slice_bitcast_fusion.table = bf16[2,400,32]{2,1,0:T(8,128)(2,1)} fusion(bf16[16,2,400,32]{3,2,1,0:T(8,128)(2,1)} %constant.24.clone, s32[]{:T(128)S(6)} %select_n.4), kind=kLoop, calls=%fused_computation | loop fusion | bytes 102404 | tf_op jit(solution)/shard_map/jit(dynamic_index_in_dim)/squeeze | solution.py:584
  6.6 0.0 copy-start
  6.6 2.4 %copy.26.state = bf16[2,768,320]{2,1,0:T(8,128)(2,1)} copy(bf16[2,768,320]{1,2,0:T(8,128)(2,1)} %param.15) | data formatting | bytes 1966080 | tf_op args[0]
  9.0 0.0 copy-done
  9.0 0.0 copy-start.1
  9.0 1.4 %copy.27.noise = bf16[2,768,320]{2,1,0:T(8,128)(2,1)} copy(bf16[2,768,320]{1,2,0:T(8,128)(2,1)S(1)} %copy-done) | data formatting | bytes 1966080 | tf_op args[1]
  10.4 0.0 copy-done.1
  10.4 1.4 %copy.28.cot = bf16[2,768,320]{2,1,0:T(8,128)(2,1)} copy(bf16[2,768,320]{1,2,0:T(8,128)(2,1)S(1)} %copy-done.1) | data formatting | bytes 1966080 | tf_op args[7]
  11.8 99.0 %block_and_gradient.1 = (bf16[2,768,320]{2,1,0:T(8,128)(2,1)}, f32[3,320]{1,0:T(4,128)}, f32[80,320]{1,0:T(8,128)}, f32[1,320]{1,0:T(1,128)}) custom-call(f32[864]{0:T(1024)} %reshape.20.filt, s32[96]{0:T(128)} %reshape.21.rows, bf16[2,768,320]{2,1,0:T(8,128)(2,1)} %copy.26.state, bf16[2,768,320]{2,1,0:T(8,128)(2,1)} %copy.27.noise, ...), custom_call_target="tpu_custom_call" | custom-call | tf_op jit(solution)/shard_map/block_and_gradient/pallas_call | solution.py:592
  110.8 0.0 copy-start.4
  110.8 0.0 copy-start.3
  110.9 0.0 copy-start.2
  110.9 2.3 %copy.29 = bf16[2,768,320]{1,2,0:T(8,128)(2,1)} copy(bf16[2,768,320]{2,1,0:T(8,128)(2,1)} %get-tuple-element.16) | data formatting | bytes 1966080
  113.2 0.0 copy-done.4
  113.2 0.6 reduce
  113.8 0.0 copy-done.3
  113.8 0.6 copy.32
  114.4 0.0 copy-done.2
  114.4 0.6 copy.33
Async XLA Ops:
  6.6 2.4 %copy-start = (bf16[2,768,320]{1,2,0:T(8,128)(2,1)S(1)}, bf16[2,768,320]{1,2,0:T(8,128)(2,1)}, u32[]{:S(2)}) copy-start(bf16[2,768,320]{1,2,0:T(8,128)(2,1)} %param.16) | copy-start | bytes 2949124
  9.0 1.4 %copy-start.1 = (bf16[2,768,320]{1,2,0:T(8,128)(2,1)S(1)}, bf16[2,768,320]{1,2,0:T(8,128)(2,1)}, u32[]{:S(2)}) copy-start(bf16[2,768,320]{1,2,0:T(8,128)(2,1)} %param.22) | copy-start | bytes 2949124
  110.8 2.4 %copy-start.4 = (f32[1,320]{1,0:T(1,128)S(1)}, f32[1,320]{1,0:T(1,128)}, u32[]{:S(2)}) copy-start(f32[1,320]{1,0:T(1,128)} %get-tuple-element.11) | copy-start | bytes 3844
  110.8 3.0 %copy-start.3 = (f32[3,320]{1,0:T(4,128)S(1)}, f32[3,320]{1,0:T(4,128)}, u32[]{:S(2)}) copy-start(f32[3,320]{1,0:T(4,128)} %get-tuple-element.25) | copy-start | bytes 11524
  110.9 3.5 %copy-start.2 = (f32[80,320]{1,0:T(8,128)S(1)}, f32[80,320]{1,0:T(8,128)}, u32[]{:S(2)}) copy-start(f32[80,320]{1,0:T(8,128)} %get-tuple-element.26) | copy-start | bytes 307204

commit v2 on v1

--- a/solution.py
+++ b/solution.py
@@ -67,9 +67,9 @@
     dims,
     filt,
     rows,
-    state,
-    noise,
-    cot,
+    state_far,
+    noise_far,
+    cot_far,
     scale,
     weight,
     gain,
@@ -84,6 +84,10 @@
     basis_out,
     gain_out,
     scale_out,
+    state,
+    noise,
+    cot,
+    field_sem,
     pad,
     gpad,
     ls,
@@ -125,6 +129,13 @@
     def source_of(off):
         return lax.rem(me - off + devices, devices)
 
+    fields = [
+        pltpu.make_async_copy(src, dst, field_sem.at[i])
+        for i, (src, dst) in enumerate(((state_far, state), (noise_far, noise), (cot_far, cot)))
+    ]
+    for copy in fields:
+        copy.start()
+
     barrier = pltpu.get_barrier_semaphore()
 
     def greet(off, z):
@@ -226,6 +237,8 @@
         return x.reshape(groups, 8, chans)
 
     sc = scale[...]
+    for copy in fields:
+        copy.wait()
     for j in range(span):
 
         def noisy(c, z):
@@ -588,6 +601,7 @@
     pick = pick.reshape(2 * each * lats, lats * SLOTS)
     vmem = pl.BlockSpec(memory_space=pltpu.VMEM)
     smem = pl.BlockSpec(memory_space=pltpu.SMEM)
+    far = pl.BlockSpec(memory_space=pl.ANY)
     dma = pltpu.SemaphoreType.DMA
     out, basis, gains, scales = pl.pallas_call(
         functools.partial(kernel, (devices, each, lons, chans, degrees, lats)),
@@ -597,9 +611,13 @@
             jax.ShapeDtypeStruct((degrees, chans), F32),
             jax.ShapeDtypeStruct((1, chans), F32),
         ),
-        in_specs=[smem, smem] + [vmem] * 13,
+        in_specs=[smem, smem] + [far] * 3 + [vmem] * 10,
         out_specs=(vmem,) * 4,
         scratch_shapes=[
+            pltpu.VMEM(state.shape, BF16),
+            pltpu.VMEM(noise.shape, BF16),
+            pltpu.VMEM(cot.shape, BF16),
+            dma((3,)),
             pltpu.VMEM((6, lons, chans), BF16),
             pltpu.VMEM((6, lons, chans), BF16),
             pltpu.VMEM((2, lons, chans), F32),

time: 115 us -> 115 us (level)
  no operation moved by 1% of the time
where the time goes in v2:
time: 115 us; the launch traced here: 114 us
  Pallas kernels  98.4 us (86%)
  local copies, waits for them, and re-layouts  14.8 us (13%)
    pallas_call x1, Pallas kernels, body(): pl.pallas_call(functools.partial(kernel, (devices, each, lons, chans, deg...  98.4 us
    unnamed x18, local copies, waits for them, and re-layouts  10.5 us

profile of v2, /device:TPU:0, one launch (start us, length us, event | category | flops | bytes accessed | tf_op | source)
XLA Modules:
  0.0 114.5 jit_solution(12918302638864529618)
XLA Ops:
  0.6 1.2 %reshape.22.scale = f32[1,320]{1,0:T(1,128)} reshape(f32[320]{0:T(512)} %param.17) | data formatting | bytes 2560 | tf_op jit(solution)/shard_map/reshape | solution.py:658
  1.9 0.8 copy.25
  2.6 0.6 reshape.21.rows
  3.3 0.9 copy.24
  4.1 0.8 reshape.20.filt
  4.9 1.6 %dynamic-slice_bitcast_fusion.table = bf16[2,400,32]{2,1,0:T(8,128)(2,1)} fusion(bf16[16,2,400,32]{3,2,1,0:T(8,128)(2,1)} %constant.24.clone, s32[]{:T(128)S(6)} %select_n.4), kind=kLoop, calls=%fused_computation | loop fusion | bytes 102404 | tf_op jit(solution)/shard_map/jit(dynamic_index_in_dim)/squeeze | solution.py:597
  6.6 0.0 copy-start
  6.6 2.4 %copy.26.state_far = bf16[2,768,320]{2,1,0:T(8,128)(2,1)} copy(bf16[2,768,320]{1,2,0:T(8,128)(2,1)} %param.15) | data formatting | bytes 1966080 | tf_op args[0]
  9.0 0.0 copy-done
  9.0 0.0 copy-start.1
  9.0 1.4 %copy.27.noise_far = bf16[2,768,320]{2,1,0:T(8,128)(2,1)} copy(bf16[2,768,320]{1,2,0:T(8,128)(2,1)S(1)} %copy-done) | data formatting | bytes 1966080 | tf_op args[1]
  10.4 0.0 copy-done.1
  10.4 1.4 %copy.28.cot_far = bf16[2,768,320]{2,1,0:T(8,128)(2,1)} copy(bf16[2,768,320]{1,2,0:T(8,128)(2,1)S(1)} %copy-done.1) | data formatting | bytes 1966080 | tf_op args[7]
  11.8 98.4 %block_and_gradient.1 = (bf16[2,768,320]{2,1,0:T(8,128)(2,1)}, f32[3,320]{1,0:T(4,128)}, f32[80,320]{1,0:T(8,128)}, f32[1,320]{1,0:T(1,128)}) custom-call(f32[864]{0:T(1024)} %reshape.20.filt, s32[96]{0:T(128)} %reshape.21.rows, bf16[2,768,320]{2,1,0:T(8,128)(2,1)} %copy.26.state_far, bf16[2,768,320]{2,1,0:T(8,128)(2,1)} %copy.27.noise_far, ...), custom_call_target="tpu_custom_call" | custom-call | tf_op jit(solution)/shard_map/block_and_gradient/pallas_call | solution.py:606
  110.3 0.0 copy-start.4
  110.3 0.0 copy-start.3
  110.3 0.0 copy-start.2
  110.3 2.3 %copy.29 = bf16[2,768,320]{1,2,0:T(8,128)(2,1)} copy(bf16[2,768,320]{2,1,0:T(8,128)(2,1)} %get-tuple-element.16) | data formatting | bytes 1966080
  112.6 0.0 copy-done.4
  112.6 0.6 reduce
  113.2 0.0 copy-done.3
  113.2 0.6 copy.32
  113.8 0.0 copy-done.2
  113.8 0.6 copy.33
Async XLA Ops:
  6.6 2.4 %copy-start = (bf16[2,768,320]{1,2,0:T(8,128)(2,1)S(1)}, bf16[2,768,320]{1,2,0:T(8,128)(2,1)}, u32[]{:S(2)}) copy-start(bf16[2,768,320]{1,2,0:T(8,128)(2,1)} %param.16) | copy-start | bytes 2949124
  9.0 1.4 %copy-start.1 = (bf16[2,768,320]{1,2,0:T(8,128)(2,1)S(1)}, bf16[2,768,320]{1,2,0:T(8,128)(2,1)}, u32[]{:S(2)}) copy-start(bf16[2,768,320]{1,2,0:T(8,128)(2,1)} %param.22) | copy-start | bytes 2949124
  110.3 2.4 %copy-start.4 = (f32[1,320]{1,0:T(1,128)S(1)}, f32[1,320]{1,0:T(1,128)}, u32[]{:S(2)}) copy-start(f32[1,320]{1,0:T(1,128)} %get-tuple-element.11) | copy-start | bytes 3844
  110.3 3.0 %copy-start.3 = (f32[3,320]{1,0:T(4,128)S(1)}, f32[3,320]{1,0:T(4,128)}, u32[]{:S(2)}) copy-start(f32[3,320]{1,0:T(4,128)} %get-tuple-element.25) | copy-start | bytes 11524
  110.3 3.5 %copy-start.2 = (f32[80,320]{1,0:T(8,128)S(1)}, f32[80,320]{1,0:T(8,128)}, u32[]{:S(2)}) copy-start(f32[80,320]{1,0:T(8,128)} %get-tuple-element.26) | copy-start | bytes 307204

commit v3 on v2

--- a/solution.py
+++ b/solution.py
@@ -247,7 +247,7 @@
             ).astype(BF16)
             return z
 
-        lax.fori_loop(0, lons // chunk, noisy, 0)
+        lax.fori_loop(0, lons // chunk, noisy, 0, unroll=4)
         send[0, :, j] = (
             dot(fwd[...], pad[2 + j]).astype(BF16).reshape(devices, SLOTS, chans)
         )
@@ -345,7 +345,7 @@
             ls[i, at(c)] = y[1].reshape(chunk, chans)
             return z
 
-        lax.fori_loop(0, lons // chunk, taps_of, 0)
+        lax.fori_loop(0, lons // chunk, taps_of, 0, unroll=4)
         ysc[0, 7:8] = ysc[0, lons + 7 : lons + 8]
         ysc[1, lons + 8 : lons + 9] = ysc[1, 8:9]
 
@@ -355,7 +355,7 @@
             )
             return z
 
-        lax.fori_loop(0, lons // chunk, join, 0)
+        lax.fori_loop(0, lons // chunk, join, 0, unroll=4)
 
     arrive(1)
 
@@ -387,7 +387,7 @@
             ysc[0, pl.ds(pl.multiple_of(8 + c * chunk, 8), chunk)] = gpad[2 + i, at(c)].astype(F32)
             return z
 
-        lax.fori_loop(0, lons // chunk, widen, 0)
+        lax.fori_loop(0, lons // chunk, widen, 0, unroll=4)
         ysc[0, 7:8] = ysc[0, lons + 7 : lons + 8]
         ysc[0, lons + 8 : lons + 9] = ysc[0, 8:9]
 
@@ -405,7 +405,7 @@
             return tuple(new)
 
         sums = lax.fori_loop(
-            0, lons // chunk, correlate, tuple(jnp.zeros((8, chans), F32) for _ in range(9))
+            0, lons // chunk, correlate, tuple(jnp.zeros((8, chans), F32) for _ in range(9)), unroll=2
         )
         for t in range(3):
             for s in range(3):
@@ -482,7 +482,7 @@
             ls[q, at(c)] = y[1].reshape(chunk, chans)
             return z
 
-        lax.fori_loop(0, lons // chunk, spread_of, 0)
+        lax.fori_loop(0, lons // chunk, spread_of, 0, unroll=4)
         ysc[0, 7:8] = ysc[0, lons + 7 : lons + 8]
         ysc[1, lons + 8 : lons + 9] = ysc[1, 8:9]
 
@@ -492,7 +492,7 @@
             )
             return z
 
-        lax.fori_loop(0, lons // chunk, join_back, 0)
+        lax.fori_loop(0, lons // chunk, join_back, 0, unroll=4)
 
     @pl.when(me < reducers)
     def _():

time: 115 us -> 114 us (level)
  no operation moved by 1% of the time
where the time goes in v3:
time: 114 us; the launch traced here: 113 us
  Pallas kernels  97.4 us (85%)
  local copies, waits for them, and re-layouts  14.8 us (13%)
    pallas_call x1, Pallas kernels, body(): pl.pallas_call(functools.partial(kernel, (devices, each, lons, chans, deg...  97.4 us
    unnamed x18, local copies, waits for them, and re-layouts  10.5 us

profile of v3, /device:TPU:0, one launch (start us, length us, event | category | flops | bytes accessed | tf_op | source)
XLA Modules:
  0.0 113.5 jit_solution(4925932124542444269)
XLA Ops:
  0.6 1.2 %reshape.22.scale = f32[1,320]{1,0:T(1,128)} reshape(f32[320]{0:T(512)} %param.17) | data formatting | bytes 2560 | tf_op jit(solution)/shard_map/reshape | solution.py:658
  1.9 0.8 copy.25
  2.6 0.6 reshape.21.rows
  3.3 0.9 copy.24
  4.1 0.8 reshape.20.filt
  4.9 1.6 %dynamic-slice_bitcast_fusion.table = bf16[2,400,32]{2,1,0:T(8,128)(2,1)} fusion(bf16[16,2,400,32]{3,2,1,0:T(8,128)(2,1)} %constant.24.clone, s32[]{:T(128)S(6)} %select_n.4), kind=kLoop, calls=%fused_computation | loop fusion | bytes 102404 | tf_op jit(solution)/shard_map/jit(dynamic_index_in_dim)/squeeze | solution.py:597
  6.6 0.0 copy-start
  6.6 2.4 %copy.26.state_far = bf16[2,768,320]{2,1,0:T(8,128)(2,1)} copy(bf16[2,768,320]{1,2,0:T(8,128)(2,1)} %param.15) | data formatting | bytes 1966080 | tf_op args[0]
  9.0 0.0 copy-done
  9.0 0.0 copy-start.1
  9.0 1.4 %copy.27.noise_far = bf16[2,768,320]{2,1,0:T(8,128)(2,1)} copy(bf16[2,768,320]{1,2,0:T(8,128)(2,1)S(1)} %copy-done) | data formatting | bytes 1966080 | tf_op args[1]
  10.4 0.0 copy-done.1
  10.4 1.4 %copy.28.cot_far = bf16[2,768,320]{2,1,0:T(8,128)(2,1)} copy(bf16[2,768,320]{1,2,0:T(8,128)(2,1)S(1)} %copy-done.1) | data formatting | bytes 1966080 | tf_op args[7]
  11.8 97.4 %block_and_gradient.1 = (bf16[2,768,320]{2,1,0:T(8,128)(2,1)}, f32[3,320]{1,0:T(4,128)}, f32[80,320]{1,0:T(8,128)}, f32[1,320]{1,0:T(1,128)}) custom-call(f32[864]{0:T(1024)} %reshape.20.filt, s32[96]{0:T(128)} %reshape.21.rows, bf16[2,768,320]{2,1,0:T(8,128)(2,1)} %copy.26.state_far, bf16[2,768,320]{2,1,0:T(8,128)(2,1)} %copy.27.noise_far, ...), custom_call_target="tpu_custom_call" | custom-call | tf_op jit(solution)/shard_map/block_and_gradient/pallas_call | solution.py:606
  109.2 0.0 copy-start.4
  109.2 0.0 copy-start.3
  109.3 0.0 copy-start.2
  109.3 2.3 %copy.29 = bf16[2,768,320]{1,2,0:T(8,128)(2,1)} copy(bf16[2,768,320]{2,1,0:T(8,128)(2,1)} %get-tuple-element.16) | data formatting | bytes 1966080
  111.6 0.0 copy-done.4
  111.6 0.6 reduce
  112.2 0.0 copy-done.3
  112.2 0.6 copy.32
  112.8 0.0 copy-done.2
  112.8 0.6 copy.33
Async XLA Ops:
  6.6 2.4 %copy-start = (bf16[2,768,320]{1,2,0:T(8,128)(2,1)S(1)}, bf16[2,768,320]{1,2,0:T(8,128)(2,1)}, u32[]{:S(2)}) copy-start(bf16[2,768,320]{1,2,0:T(8,128)(2,1)} %param.16) | copy-start | bytes 2949124
  9.0 1.4 %copy-start.1 = (bf16[2,768,320]{1,2,0:T(8,128)(2,1)S(1)}, bf16[2,768,320]{1,2,0:T(8,128)(2,1)}, u32[]{:S(2)}) copy-start(bf16[2,768,320]{1,2,0:T(8,128)(2,1)} %param.22) | copy-start | bytes 2949124
  109.2 2.4 %copy-start.4 = (f32[1,320]{1,0:T(1,128)S(1)}, f32[1,320]{1,0:T(1,128)}, u32[]{:S(2)}) copy-start(f32[1,320]{1,0:T(1,128)} %get-tuple-element.11) | copy-start | bytes 3844
  109.2 3.0 %copy-start.3 = (f32[3,320]{1,0:T(4,128)S(1)}, f32[3,320]{1,0:T(4,128)}, u32[]{:S(2)}) copy-start(f32[3,320]{1,0:T(4,128)} %get-tuple-element.25) | copy-start | bytes 11524
  109.3 3.5 %copy-start.2 = (f32[80,320]{1,0:T(8,128)S(1)}, f32[80,320]{1,0:T(8,128)}, u32[]{:S(2)}) copy-start(f32[80,320]{1,0:T(8,128)} %get-tuple-element.26) | copy-start | bytes 307204
